TPU v7x, 32 devices: a whole 2x2x4 slice. The times are simulated.
32 devices in a mesh: dp: 2 (over core), row: 4 (over y, x), col: 4 (over z).
Axes of the slice: x: 2, y: 2, z: 4, core: 2. Of those that a mesh axis runs over, the one named last changes fastest.
Arguments:
- states: float32 [5120, 1024], P(('dp', 'row'), 'col'), may hold values from -6 to 6
- teacher: bfloat16 [5120, 1024], P(('dp', 'row'), 'col'), may hold values from -6 to 6
- cotangent: float32 [5120, 1024], P(('dp', 'row'), 'col'), may hold values from -6 to 6
- lengths: int32 [16], P(('dp', 'row')), may hold values from 256 to 320
- norm_gain: float32 [2, 2, 1024], P(None, None, 'col'), may hold values from 0.5 to 1.5
- norm_bias: float32 [2, 2, 1024], P(None, None, 'col'), may hold values from -2 to 2
- in_weight: bfloat16 [2, 1024, 3, 1024], P(None, 'row', None, 'col'), may hold values from -0.1875 to 0.1875
- in_bias: float32 [2, 2, 1024], P(None, None, 'col'), may hold values from -2 to 2
- proj_weight: bfloat16 [2, 1024, 1024], P(None, 'col', 'row'), may hold values from -0.75 to 0.75
- proj_bias: float32 [2, 1024], P(None, 'col'), may hold values from -2 to 2
- up_weight: bfloat16 [2, 1024, 4096], P(None, 'row', 'col'), may hold values from -0.1875 to 0.1875
- up_bias: float32 [2, 4096], P(None, 'col'), may hold values from -2 to 2
- down_weight: bfloat16 [2, 4096, 1024], P(None, 'col', 'row'), may hold values from -0.125 to 0.125
- down_bias: float32 [2, 1024], P(None, 'col'), may hold values from -2 to 2
Outputs:
- loss_value: float32 [], replicated
- output: float32 [5120, 1024], P(('dp', 'row'), 'col')
- input_grad: float32 [5120, 1024], P(('dp', 'row'), 'col')
- norm_gain_grad: float32 [2, 2, 1024], P(None, None, 'col')
- norm_bias_grad: float32 [2, 2, 1024], P(None, None, 'col')
- in_weight_grad: float32 [2, 1024, 3, 1024], P(None, 'row', None, 'col')
- in_bias_grad: float32 [2, 2, 1024], P(None, None, 'col')
- proj_weight_grad: float32 [2, 1024, 1024], P(None, 'col', 'row')
- proj_bias_grad: float32 [2, 1024], P(None, 'col')
- up_weight_grad: float32 [2, 1024, 4096], P(None, 'row', 'col')
- up_bias_grad: float32 [2, 4096], P(None, 'col')
- down_weight_grad: float32 [2, 4096, 1024], P(None, 'col', 'row')
- down_bias_grad: float32 [2, 1024], P(None, 'col')
Inputs may be any that keep to these rules, and one draw needn't show every extreme that they name: `lengths`: number of valid slots of a sequence; slots from that number on are padding.
All inputs are finite; a program needn't handle non-finite values.
Results may differ from a plain program's by a relative error of at most 0.013.
Values may be sent and summed in bfloat16 or wider, within the bound.
No kernel may reach another device: no remote copies, remote signals or barrier semaphores. Data moves between devices by JAX's collectives and lax.ppermute only.
A program may use at most 192 MiB of HBM per device.

v0:
```python
import jax
import jax.numpy as jnp
from jax import lax
from jax.sharding import PartitionSpec as P

HEAD_DIM = 64
LAYERS = 2
epsilon = 1e-06
fill_value = -1e30


def gelu_exact(inputs):
    return jax.nn.gelu(inputs, approximate=False)


def feature_rows(partial_value):
    return lax.psum_scatter(partial_value, "col", scatter_dimension=1, tiled=True)


def gradient_rows(partial_value):
    return lax.psum_scatter(
        partial_value.astype(jnp.bfloat16), "col", scatter_dimension=1, tiled=True
    ).astype(jnp.float32)


def gather_gradient(gradient):
    return lax.all_gather(gradient, "col", axis=1, tiled=True)


def norm_shares(inputs, gains, shifts, model_width):
    totals = lax.psum((jnp.sum(inputs, axis=1), jnp.sum(inputs * inputs, axis=1)), "col")
    centre = (totals[0] / model_width)[:, None]
    rscale = lax.rsqrt((totals[1] / model_width)[:, None] - centre * centre + epsilon)
    standard = (inputs - centre) * rscale
    normed = lax.all_gather(
        (standard * gains + shifts).astype(jnp.bfloat16), "col", axis=1, tiled=True
    )
    return (normed, standard, rscale)


def norm_backward(grad_share, standard, rscale, gains, model_width):
    scaled = grad_share * gains
    sums = lax.psum((jnp.sum(scaled, axis=1), jnp.sum(scaled * standard, axis=1)), "col")
    grad_input = rscale * (
        scaled - sums[0][:, None] / model_width - standard * sums[1][:, None] / model_width
    )
    return (grad_input, jnp.sum(grad_share * standard, axis=0), jnp.sum(grad_share, axis=0))


def split_heads(flat_rows, seq_here):
    return flat_rows.reshape(
        seq_here, flat_rows.shape[0] // seq_here, flat_rows.shape[1] // HEAD_DIM, HEAD_DIM
    )


def attention_scores(queries, key_block, validity, score_scale):
    scores = (
        jnp.einsum("sqhe,skhe->shqk", queries, key_block, preferred_element_type=jnp.float32)
        * score_scale
    )
    return jnp.where(validity[:, None, None, :], scores, fill_value)


def attend(queries, key_block, values, validity, score_scale):
    scores = attention_scores(queries, key_block, validity, score_scale)
    maximum = jnp.max(scores, axis=-1, keepdims=True)
    exponent = jnp.exp(scores - maximum)
    total_mass = jnp.sum(exponent, axis=-1, keepdims=True)
    attention = (exponent / total_mass).astype(jnp.bfloat16)
    mixture = jnp.einsum("shqk,skhe->sqhe", attention, values, preferred_element_type=jnp.float32)
    return (mixture, maximum + jnp.log(total_mass))


def attend_back(queries, key_block, values, validity, score_scale, logsum, grad_mixture):
    scores = attention_scores(queries, key_block, validity, score_scale)
    chance = jnp.exp(scores - logsum)
    grad_values = jnp.einsum(
        "shqk,sqhe->skhe",
        chance.astype(jnp.bfloat16),
        grad_mixture,
        preferred_element_type=jnp.float32,
    )
    grad_chance = jnp.einsum(
        "sqhe,skhe->shqk", grad_mixture, values, preferred_element_type=jnp.float32
    )
    grad_scores = (
        chance * (grad_chance - jnp.sum(grad_chance * chance, axis=-1, keepdims=True))
    ).astype(jnp.bfloat16)
    grad_queries = (
        jnp.einsum("shqk,skhe->sqhe", grad_scores, key_block, preferred_element_type=jnp.float32)
        * score_scale
    )
    grad_keys = (
        jnp.einsum("shqk,sqhe->skhe", grad_scores, queries, preferred_element_type=jnp.float32)
        * score_scale
    )
    return (grad_queries, grad_keys, grad_values)


def body(
    states,
    teacher,
    cotangent,
    lengths,
    norm_gain,
    norm_bias,
    in_weight,
    in_bias,
    proj_weight,
    proj_bias,
    up_weight,
    up_bias,
    down_weight,
    down_bias,
):
    token_rows = states.shape[0]
    share_width = states.shape[1]
    model_width = share_width * lax.axis_size("col")
    seq_here = lengths.shape[0]
    slot_count = token_rows // seq_here
    score_scale = HEAD_DIM ** (-0.5)
    positions = jnp.arange(slot_count, dtype=jnp.int32)
    validity = positions[None, :] < lengths[:, None]
    row_mask = validity.reshape(token_rows, 1).astype(jnp.float32)
    current = states
    records = []
    for layer_index in range(LAYERS):
        fetched = (
            lax.all_gather(in_weight[layer_index], "row", axis=0, tiled=True),
            lax.all_gather(proj_weight[layer_index], "row", axis=1, tiled=True),
            lax.all_gather(up_weight[layer_index], "row", axis=0, tiled=True),
            lax.all_gather(down_weight[layer_index], "row", axis=1, tiled=True),
        )
        in_full, proj_full, up_full, down_full = fetched
        normed_one, standard_one, rscale_one = norm_shares(
            current, norm_gain[layer_index, 0], norm_bias[layer_index, 0], model_width
        )
        projected = jnp.einsum(
            "td,dpe->tpe", normed_one, in_full, preferred_element_type=jnp.float32
        )
        queries = split_heads(
            (projected[:, 0] + in_bias[layer_index, 0]).astype(jnp.bfloat16), seq_here
        )
        key_block = split_heads(projected[:, 1].astype(jnp.bfloat16), seq_here)
        values = split_heads(
            (projected[:, 2] + in_bias[layer_index, 1]).astype(jnp.bfloat16), seq_here
        )
        mixture, logsum = attend(queries, key_block, values, validity, score_scale)
        attended = mixture.reshape(token_rows, share_width).astype(jnp.bfloat16)
        attn_partial = jnp.dot(attended, proj_full, preferred_element_type=jnp.float32)
        middle = current + feature_rows(attn_partial) + proj_bias[layer_index]
        normed_two, standard_two, rscale_two = norm_shares(
            middle, norm_gain[layer_index, 1], norm_bias[layer_index, 1], model_width
        )
        hidden_pre = (
            jnp.dot(normed_two, up_full, preferred_element_type=jnp.float32) + up_bias[layer_index]
        )
        hidden = gelu_exact(hidden_pre).astype(jnp.bfloat16)
        down_partial = jnp.dot(hidden, down_full, preferred_element_type=jnp.float32)
        records.append(
            (
                fetched,
                normed_one,
                standard_one,
                rscale_one,
                queries,
                key_block,
                values,
                logsum,
                attended,
                normed_two,
                standard_two,
                rscale_two,
                hidden_pre,
                hidden,
            )
        )
        branch = feature_rows(down_partial) + down_bias[layer_index]
        current = (middle + branch) * row_mask
    residue = current - teacher.astype(jnp.float32)
    local_squared = jnp.sum(residue * residue * row_mask)
    local_count = jnp.where(lax.axis_index("col") == 0, jnp.sum(row_mask), 0.0)
    token_total, squared_total = lax.psum((local_count, local_squared), ("dp", "row", "col"))
    loss_value = squared_total / (token_total * model_width)
    factor = token_rows * lax.axis_size("dp") * lax.axis_size("row") / token_total
    grad_current = cotangent + 2.0 * factor * residue * row_mask
    results = [None] * LAYERS
    for layer_index in reversed(range(LAYERS)):
        (
            fetched,
            normed_one,
            standard_one,
            rscale_one,
            queries,
            key_block,
            values,
            logsum,
            attended,
            normed_two,
            standard_two,
            rscale_two,
            hidden_pre,
            hidden,
        ) = records[layer_index]
        in_full, proj_full, up_full, down_full = fetched
        grad_two = grad_current * row_mask
        grad_two_low = grad_two.astype(jnp.bfloat16)
        down_bias_part = jnp.sum(grad_two_low.astype(jnp.float32), axis=0)
        grad_two_rows = gather_gradient(grad_two_low)
        down_part = jnp.einsum(
            "tf,td->fd", hidden, grad_two_rows, preferred_element_type=jnp.float32
        )
        grad_hidden = jnp.einsum(
            "td,fd->tf", grad_two_rows, down_full, preferred_element_type=jnp.float32
        )
        ignored, gelu_pull = jax.vjp(gelu_exact, hidden_pre)
        grad_pre_low = gelu_pull(grad_hidden)[0].astype(jnp.bfloat16)
        up_bias_part = jnp.sum(grad_pre_low.astype(jnp.float32), axis=0)
        up_part = jnp.einsum(
            "td,tf->df", normed_two, grad_pre_low, preferred_element_type=jnp.float32
        )
        grad_normed_two = gradient_rows(
            jnp.einsum("tf,df->td", grad_pre_low, up_full, preferred_element_type=jnp.float32)
        )
        grad_norm_two, gain_part_two, shift_part_two = norm_backward(
            grad_normed_two, standard_two, rscale_two, norm_gain[layer_index, 1], model_width
        )
        grad_middle = grad_two + grad_norm_two
        grad_one_low = grad_middle.astype(jnp.bfloat16)
        proj_bias_part = jnp.sum(grad_one_low.astype(jnp.float32), axis=0)
        grad_one_rows = gather_gradient(grad_one_low)
        proj_part = jnp.einsum(
            "te,td->ed", attended, grad_one_rows, preferred_element_type=jnp.float32
        )
        grad_attended = jnp.einsum(
            "td,ed->te", grad_one_rows, proj_full, preferred_element_type=jnp.float32
        ).astype(jnp.bfloat16)
        grad_queries, grad_keys, grad_values = attend_back(
            queries,
            key_block,
            values,
            validity,
            score_scale,
            logsum,
            split_heads(grad_attended, seq_here),
        )
        grad_triple = jnp.stack(
            [
                grad_queries.reshape(token_rows, share_width),
                grad_keys.reshape(token_rows, share_width),
                grad_values.reshape(token_rows, share_width),
            ],
            axis=1,
        ).astype(jnp.bfloat16)
        in_part = jnp.einsum(
            "td,tpe->dpe", normed_one, grad_triple, preferred_element_type=jnp.float32
        )
        in_bias_part = jnp.stack(
            [
                jnp.sum(grad_triple[:, 0].astype(jnp.float32), axis=0),
                jnp.sum(grad_triple[:, 2].astype(jnp.float32), axis=0),
            ]
        )
        grad_normed_one = gradient_rows(
            jnp.einsum("tpe,dpe->td", grad_triple, in_full, preferred_element_type=jnp.float32)
        )
        grad_norm_one, gain_part_one, shift_part_one = norm_backward(
            grad_normed_one, standard_one, rscale_one, norm_gain[layer_index, 0], model_width
        )
        grad_current = grad_middle + grad_norm_one
        blocks = (
            lax.psum_scatter(
                in_part.astype(jnp.bfloat16), "row", scatter_dimension=0, tiled=True
            ).astype(jnp.float32),
            lax.psum_scatter(
                proj_part.astype(jnp.bfloat16), "row", scatter_dimension=1, tiled=True
            ).astype(jnp.float32),
            lax.psum_scatter(
                up_part.astype(jnp.bfloat16), "row", scatter_dimension=0, tiled=True
            ).astype(jnp.float32),
            lax.psum_scatter(
                down_part.astype(jnp.bfloat16), "row", scatter_dimension=1, tiled=True
            ).astype(jnp.float32),
        )
        blocks = (
            lax.psum(blocks[0].astype(jnp.bfloat16), "dp").astype(jnp.float32),
            lax.psum(blocks[1].astype(jnp.bfloat16), "dp").astype(jnp.float32),
            lax.psum(blocks[2].astype(jnp.bfloat16), "dp").astype(jnp.float32),
            lax.psum(blocks[3].astype(jnp.bfloat16), "dp").astype(jnp.float32),
        )
        vectors = lax.psum(
            (
                jnp.stack([gain_part_one, gain_part_two]),
                jnp.stack([shift_part_one, shift_part_two]),
                in_bias_part,
                proj_bias_part,
                up_bias_part,
                down_bias_part,
            ),
            ("dp", "row"),
        )
        results[layer_index] = (
            vectors[0],
            vectors[1],
            blocks[0],
            vectors[2],
            blocks[1],
            vectors[3],
            blocks[2],
            vectors[4],
            blocks[3],
            vectors[5],
        )
    stacked = [
        jnp.stack([results[layer_index][member] for layer_index in range(LAYERS)])
        for member in range(10)
    ]
    return (
        loss_value,
        current,
        grad_current,
        stacked[0],
        stacked[1],
        stacked[2],
        stacked[3],
        stacked[4],
        stacked[5],
        stacked[6],
        stacked[7],
        stacked[8],
        stacked[9],
    )


def solution(mesh):
    in_specs = (
        P(("dp", "row"), "col"),
        P(("dp", "row"), "col"),
        P(("dp", "row"), "col"),
        P(("dp", "row")),
        P(None, None, "col"),
        P(None, None, "col"),
        P(None, "row", None, "col"),
        P(None, None, "col"),
        P(None, "col", "row"),
        P(None, "col"),
        P(None, "row", "col"),
        P(None, "col"),
        P(None, "col", "row"),
        P(None, "col"),
    )
    out_specs = (
        P(),
        P(("dp", "row"), "col"),
        P(("dp", "row"), "col"),
        P(None, None, "col"),
        P(None, None, "col"),
        P(None, "row", None, "col"),
        P(None, None, "col"),
        P(None, "col", "row"),
        P(None, "col"),
        P(None, "row", "col"),
        P(None, "col"),
        P(None, "col", "row"),
        P(None, "col"),
    )
    return jax.shard_map(body, mesh=mesh, in_specs=in_specs, out_specs=out_specs, check_vma=False)
```

profile of v0, /device:TPU:0, one launch (start us, length us, event | category | flops | bytes accessed | tf_op | source)
XLA Modules:
  0.0 1360.7 jit_solution(17156937366289661022)
XLA Ops:
  11.2 13.7 %all-reduce.9 = (f32[640]{0:T(1024)S(1)}, f32[640]{0:T(1024)S(1)}) all-reduce(f32[640]{0:T(1024)S(1)} %get-tuple-element.28, f32[640]{0:T(1024)S(1)} %get-tuple-element.27), channel_id=1, replica_groups=mesh['dp'=2,'row'=4,'col'=4] {'col'}, use_global_device_ids=true, to_apply=%region_3.0 | all-reduce | flops 1280 | bytes 10240 | tf_op jit(solution)/shard_map/psum | solution.py:31
  30.7 12.9 all-gather.1
  44.3 14.6 %all-gather.23.cloned.1.call-done = bf16[640,1024]{1,0:T(8,128)(2,1)} async-done(((bf16[640,256]{1,0:T(8,128)(2,1)}), bf16[640,1024]{1,0:T(8,128)(2,1)}) %all-gather.23.cloned.1.call-update) | async-done | bytes 1310736 | tf_op jit(solution)/shard_map/all_gather | solution.py:35
  58.9 32.0 %all-gather.39.cloned.1.call-done = bf16[1,1024,3,256]{3,1,2,0:T(8,128)(2,1)} async-done(((bf16[1,256,3,256]{3,1,2,0:T(8,128)(2,1)}), bf16[1,1024,3,256]{3,1,2,0:T(8,128)(2,1)}) %all-gather.39.cloned.1.call-update) | async-done | bytes 1572880 | tf_op jit(solution)/shard_map/all_gather | solution.py:129
  107.8 50.5 %reduce-scatter.17.cloned.1.call-done = f32[640,256]{1,0:T(8,128)} async-done(((f32[640,1024]{1,0:T(8,128)}), f32[640,256]{1,0:T(8,128)}) %reduce-scatter.17.cloned.1.call-update) | async-done | bytes 655376 | tf_op jit(solution)/shard_map/reduce_scatter | solution.py:17
  174.1 21.4 %all-gather.41.cloned.1.call-done = bf16[1,1024,1024]{2,1,0:T(8,128)(2,1)} async-done(((bf16[1,256,1024]{2,1,0:T(8,128)(2,1)}), bf16[1,1024,1024]{2,1,0:T(8,128)(2,1)}) %all-gather.41.cloned.1.call-update) | async-done | bytes 2097168 | tf_op jit(solution)/shard_map/all_gather | solution.py:131
  195.5 35.5 %all-gather.25.cloned.1.call-done = bf16[640,1024]{1,0:T(8,128)(2,1)} async-done(((bf16[640,256]{1,0:T(8,128)(2,1)}), bf16[640,1024]{1,0:T(8,128)(2,1)}) %all-gather.25.cloned.1.call-update) | async-done | bytes 1310736 | tf_op jit(solution)/shard_map/all_gather | solution.py:35
  241.3 25.7 %all-gather.43.cloned.1.call-done = bf16[1,1024,1024]{2,1,0:T(8,128)(2,1)} async-done(((bf16[1,1024,256]{2,1,0:T(8,128)(2,1)}), bf16[1,1024,1024]{2,1,0:T(8,128)(2,1)}) %all-gather.43.cloned.1.call-update) | async-done | bytes 2097168 | tf_op jit(solution)/shard_map/all_gather | solution.py:132
  273.6 50.8 %reduce-scatter.19.cloned.1.call-done = f32[640,256]{1,0:T(8,128)} async-done(((f32[640,1024]{1,0:T(8,128)}), f32[640,256]{1,0:T(8,128)}) %reduce-scatter.19.cloned.1.call-update) | async-done | bytes 655376 | tf_op jit(solution)/shard_map/reduce_scatter | solution.py:17
  338.6 16.2 %all-gather.5 = bf16[1,256,1024]{2,1,0:T(8,128)(2,1)} all-gather(bf16[1,256,256]{2,1,0:T(8,128)(2,1)S(1)} %copy-done.32), channel_id=7, replica_groups=mesh['dp'=2,'row'=4,'col'=4] {'row'}, dimensions={2}, use_global_device_ids=true | all-gather | bytes 655360 | tf_op jit(solution)/shard_map/all_gather | solution.py:130
  360.5 34.8 %all-gather.27.cloned.1.call-done = bf16[640,1024]{1,0:T(8,128)(2,1)} async-done(((bf16[640,256]{1,0:T(8,128)(2,1)}), bf16[640,1024]{1,0:T(8,128)(2,1)}) %all-gather.27.cloned.1.call-update) | async-done | bytes 1310736 | tf_op jit(solution)/shard_map/all_gather | solution.py:35
  422.2 50.0 %reduce-scatter.21.cloned.1.call-done = f32[640,256]{1,0:T(8,128)} async-done(((f32[640,1024]{1,0:T(8,128)}), f32[640,256]{1,0:T(8,128)}) %reduce-scatter.21.cloned.1.call-update) | async-done | bytes 655376 | tf_op jit(solution)/shard_map/reduce_scatter | solution.py:17
  486.1 23.5 %all-gather.47.cloned.1.call-done = bf16[1,1024,1024]{2,1,0:T(8,128)(2,1)} async-done(((bf16[1,256,1024]{2,1,0:T(8,128)(2,1)}), bf16[1,1024,1024]{2,1,0:T(8,128)(2,1)}) %all-gather.47.cloned.1.call-update) | async-done | bytes 2097168 | tf_op jit(solution)/shard_map/all_gather | solution.py:131
  509.7 35.5 %all-gather.29.cloned.1.call-done = bf16[640,1024]{1,0:T(8,128)(2,1)} async-done(((bf16[640,256]{1,0:T(8,128)(2,1)}), bf16[640,1024]{1,0:T(8,128)(2,1)}) %all-gather.29.cloned.1.call-update) | async-done | bytes 1310736 | tf_op jit(solution)/shard_map/all_gather | solution.py:35
  555.4 25.9 %all-gather.49.cloned.1.call-done = bf16[1,1024,1024]{2,1,0:T(8,128)(2,1)} async-done(((bf16[1,1024,256]{2,1,0:T(8,128)(2,1)}), bf16[1,1024,1024]{2,1,0:T(8,128)(2,1)}) %all-gather.49.cloned.1.call-update) | async-done | bytes 2097168 | tf_op jit(solution)/shard_map/all_gather | solution.py:132
  588.2 50.3 %reduce-scatter.23.cloned.1.call-done = f32[640,256]{1,0:T(8,128)} async-done(((f32[640,1024]{1,0:T(8,128)}), f32[640,256]{1,0:T(8,128)}) %reduce-scatter.23.cloned.1.call-update) | async-done | bytes 655376 | tf_op jit(solution)/shard_map/reduce_scatter | solution.py:17
  641.4 40.1 %all-reduce = (f32[]{:T(128)}, f32[]{:T(128)}) all-reduce(f32[]{:T(128)} %get-tuple-element.90, f32[]{:T(128)S(6)} %select_n.15), channel_id=1, replica_groups=mesh['dp'=2,'row'=4,'col'=4] {'dp','row','col'}, use_global_device_ids=true, to_apply=%region_25.26 | all-reduce | flops 2 | bytes 16 | tf_op jit(solution)/shard_map/psum | solution.py:183
  684.6 33.5 %all-gather.31.cloned.1.call-done = bf16[640,1024]{1,0:T(8,128)(2,1)} async-done(((bf16[640,256]{1,0:T(8,128)(2,1)}), bf16[640,1024]{1,0:T(8,128)(2,1)}) %all-gather.31.cloned.1.call-update) | async-done | bytes 1310736 | tf_op jit(solution)/shard_map/all_gather | solution.py:27
  727.9 29.8 %reduce-scatter.25.cloned.1.call-done = bf16[640,256]{1,0:T(8,128)(2,1)} async-done(((bf16[640,1024]{1,0:T(8,128)(2,1)}), bf16[640,256]{1,0:T(8,128)(2,1)}) %reduce-scatter.25.cloned.1.call-update) | async-done | bytes 327696 | tf_op jit(solution)/shard_map/reduce_scatter | solution.py:21
  772.1 31.7 %all-gather.33.cloned.1.call-done = bf16[640,1024]{1,0:T(8,128)(2,1)} async-done(((bf16[640,256]{1,0:T(8,128)(2,1)}), bf16[640,1024]{1,0:T(8,128)(2,1)}) %all-gather.33.cloned.1.call-update) | async-done | bytes 1310736 | tf_op jit(solution)/shard_map/all_gather | solution.py:27
  831.2 29.9 %reduce-scatter.27.cloned.1.call-done = bf16[640,256]{1,0:T(8,128)(2,1)} async-done(((bf16[640,1024]{1,0:T(8,128)(2,1)}), bf16[640,256]{1,0:T(8,128)(2,1)}) %reduce-scatter.27.cloned.1.call-update) | async-done | bytes 327696 | tf_op jit(solution)/shard_map/reduce_scatter | solution.py:21
  875.0 31.7 %all-gather.35.cloned.1.call-done = bf16[640,1024]{1,0:T(8,128)(2,1)} async-done(((bf16[640,256]{1,0:T(8,128)(2,1)}), bf16[640,1024]{1,0:T(8,128)(2,1)}) %all-gather.35.cloned.1.call-update) | async-done | bytes 1310736 | tf_op jit(solution)/shard_map/all_gather | solution.py:27
  916.6 29.9 %reduce-scatter.29.cloned.1.call-done = bf16[640,256]{1,0:T(8,128)(2,1)} async-done(((bf16[640,1024]{1,0:T(8,128)(2,1)}), bf16[640,256]{1,0:T(8,128)(2,1)}) %reduce-scatter.29.cloned.1.call-update) | async-done | bytes 327696 | tf_op jit(solution)/shard_map/reduce_scatter | solution.py:21
  1028.7 39.0 %reduce-scatter.43.cloned.1.call-done = bf16[256,1024]{1,0:T(8,128)(2,1)} async-done(((bf16[1024,1024]{1,0:T(8,128)(2,1)}), bf16[256,1024]{1,0:T(8,128)(2,1)}) %reduce-scatter.43.cloned.1.call-update) | async-done | bytes 524304 | tf_op jit(solution)/shard_map/reduce_scatter | solution.py:278
  1067.8 28.1 %reduce-scatter.39.cloned.1.call-done = bf16[256,256]{1,0:T(8,128)(2,1)} async-done(((bf16[256,1024]{1,0:T(8,128)(2,1)}), bf16[256,256]{1,0:T(8,128)(2,1)}) %reduce-scatter.39.cloned.1.call-update) | async-done | bytes 131088 | tf_op jit(solution)/shard_map/reduce_scatter | solution.py:275
  1095.8 34.8 %reduce-scatter.35.cloned.1.call-done = bf16[256,3,256]{2,0,1:T(8,128)(2,1)} async-done(((bf16[1024,3,256]{2,0,1:T(8,128)(2,1)}), bf16[256,3,256]{2,0,1:T(8,128)(2,1)}) %reduce-scatter.35.cloned.1.call-update) | async-done | bytes 393232 | tf_op jit(solution)/shard_map/reduce_scatter | solution.py:272
  1130.6 38.3 %reduce-scatter.45.cloned.1.call-done = bf16[1024,256]{1,0:T(8,128)(2,1)} async-done(((bf16[1024,1024]{1,0:T(8,128)(2,1)}), bf16[1024,256]{1,0:T(8,128)(2,1)}) %reduce-scatter.45.cloned.1.call-update) | async-done | bytes 524304 | tf_op jit(solution)/shard_map/reduce_scatter | solution.py:281
  1168.9 38.6 %reduce-scatter.41.cloned.1.call-done = bf16[256,1024]{1,0:T(8,128)(2,1)} async-done(((bf16[1024,1024]{1,0:T(8,128)(2,1)}), bf16[256,1024]{1,0:T(8,128)(2,1)}) %reduce-scatter.41.cloned.1.call-update) | async-done | bytes 524304 | tf_op jit(solution)/shard_map/reduce_scatter | solution.py:278
  1207.5 27.9 %reduce-scatter.37.cloned.1.call-done = bf16[256,256]{1,0:T(8,128)(2,1)} async-done(((bf16[256,1024]{1,0:T(8,128)(2,1)}), bf16[256,256]{1,0:T(8,128)(2,1)}) %reduce-scatter.37.cloned.1.call-update) | async-done | bytes 131088 | tf_op jit(solution)/shard_map/reduce_scatter | solution.py:275
  1235.4 34.0 %reduce-scatter.33.cloned.1.call-done = bf16[256,3,256]{2,0,1:T(8,128)(2,1)} async-done(((bf16[1024,3,256]{2,0,1:T(8,128)(2,1)}), bf16[256,3,256]{2,0,1:T(8,128)(2,1)}) %reduce-scatter.33.cloned.1.call-update) | async-done | bytes 393232 | tf_op jit(solution)/shard_map/reduce_scatter | solution.py:272
  1271.3 31.4 %reduce-scatter.31.cloned.1.call-done = bf16[640,256]{1,0:T(8,128)(2,1)} async-done(((bf16[640,1024]{1,0:T(8,128)(2,1)}), bf16[640,256]{1,0:T(8,128)(2,1)}) %reduce-scatter.31.cloned.1.call-update) | async-done | bytes 327696 | tf_op jit(solution)/shard_map/reduce_scatter | solution.py:21
  1304.2 26.5 %all-reduce.1 = (f32[1,2,256]{2,1,0:T(2,128)S(1)}, f32[1,2,256]{2,1,0:T(2,128)S(1)}, f32[1,2,256]{2,1,0:T(2,128)S(1)}, f32[1,2,256]{2,1,0:T(2,128)S(1)}, f32[1,2...) all-reduce(f32[1,2,256]{2,1,0:T(2,128)S(1)} %maximum_bitcast_fusion, ...), channel_id=1, replica_groups=mesh['dp'=2,'row'=4,'col'=4] {'dp','row'}, use_global_device_ids=true, to_apply=%region_55.56 | all-reduce | flops 6144 | bytes 49152 | tf_op jit(solution)/shard_map/psum | solution.py:291
  (410 shorter events, 322.1 us)
Async XLA Ops:
  7.2 51.7 %all-gather.23.cloned.1.call-start = ((), (), s32[]{:S(2)}) async-start(), calls=%async_computation.16 | async-start | bytes 1638400 | tf_op jit(solution)/shard_map/all_gather | solution.py:35
  27.1 63.8 %all-gather.39.cloned.1.call-start = ((), (), s32[]{:S(2)}) async-start(), calls=%async_computation.40 | async-start | bytes 1966080 | tf_op jit(solution)/shard_map/all_gather | solution.py:129
  29.2 129.1 %reduce-scatter.17.cloned.1.call-start = ((), (), s32[]{:S(2)}) async-start(), calls=%async_computation.17 | async-start | bytes 3276800 | tf_op jit(solution)/shard_map/reduce_scatter | solution.py:17
  106.0 89.5 %all-gather.41.cloned.1.call-start = ((), (), s32[]{:S(2)}) async-start(), calls=%async_computation.41 | async-start | bytes 2621440 | tf_op jit(solution)/shard_map/all_gather | solution.py:131
  107.1 123.9 %all-gather.25.cloned.1.call-start = ((), (), s32[]{:S(2)}) async-start(), calls=%async_computation.18 | async-start | bytes 1638400 | tf_op jit(solution)/shard_map/all_gather | solution.py:35
  170.9 96.1 %all-gather.43.cloned.1.call-start = ((), (), s32[]{:S(2)}) async-start(), calls=%async_computation.42 | async-start | bytes 2621440 | tf_op jit(solution)/shard_map/all_gather | solution.py:132
  173.2 151.2 %reduce-scatter.19.cloned.1.call-start = ((), (), s32[]{:S(2)}) async-start(), calls=%async_computation.19 | async-start | bytes 3276800 | tf_op jit(solution)/shard_map/reduce_scatter | solution.py:17
  272.1 88.4 %all-gather.45.cloned.1.call-start = ((), (), s32[]{:S(2)}) async-start(), calls=%async_computation.43 | async-start | bytes 1966080 | tf_op jit(solution)/shard_map/all_gather | solution.py:129
  272.9 122.4 %all-gather.27.cloned.1.call-start = ((), (), s32[]{:S(2)}) async-start(), calls=%async_computation.20 | async-start | bytes 1638400 | tf_op jit(solution)/shard_map/all_gather | solution.py:35
  337.2 135.0 %reduce-scatter.21.cloned.1.call-start = ((), (), s32[]{:S(2)}) async-start(), calls=%async_computation.21 | async-start | bytes 3276800 | tf_op jit(solution)/shard_map/reduce_scatter | solution.py:17
  421.4 88.2 %all-gather.47.cloned.1.call-start = ((), (), s32[]{:S(2)}) async-start(), calls=%async_computation.44 | async-start | bytes 2621440 | tf_op jit(solution)/shard_map/all_gather | solution.py:131
  422.2 123.0 %all-gather.29.cloned.1.call-start = ((), (), s32[]{:S(2)}) async-start(), calls=%async_computation.22 | async-start | bytes 1638400 | tf_op jit(solution)/shard_map/all_gather | solution.py:35
  484.9 96.4 %all-gather.49.cloned.1.call-start = ((), (), s32[]{:S(2)}) async-start(), calls=%async_computation.45 | async-start | bytes 2621440 | tf_op jit(solution)/shard_map/all_gather | solution.py:132
  485.6 152.9 %reduce-scatter.23.cloned.1.call-start = ((), (), s32[]{:S(2)}) async-start(), calls=%async_computation.23 | async-start | bytes 3276800 | tf_op jit(solution)/shard_map/reduce_scatter | solution.py:17
  586.2 131.8 %all-gather.31.cloned.1.call-start = ((), (), s32[]{:S(2)}) async-start(), calls=%async_computation.24 | async-start | bytes 1638400 | tf_op jit(solution)/shard_map/all_gather | solution.py:27
  684.5 73.3 %reduce-scatter.25.cloned.1.call-start = ((), (), s32[]{:S(2)}) async-start(), calls=%async_computation.25 | async-start | bytes 1638400 | tf_op jit(solution)/shard_map/reduce_scatter | solution.py:21
  727.9 76.0 %all-gather.33.cloned.1.call-start = ((), (), s32[]{:S(2)}) async-start(), calls=%async_computation.26 | async-start | bytes 1638400 | tf_op jit(solution)/shard_map/all_gather | solution.py:27
  771.8 89.3 %reduce-scatter.27.cloned.1.call-start = ((), (), s32[]{:S(2)}) async-start(), calls=%async_computation.27 | async-start | bytes 1638400 | tf_op jit(solution)/shard_map/reduce_scatter | solution.py:21
  831.2 75.5 %all-gather.35.cloned.1.call-start = ((), (), s32[]{:S(2)}) async-start(), calls=%async_computation.28 | async-start | bytes 1638400 | tf_op jit(solution)/shard_map/all_gather | solution.py:27
  874.7 71.8 %reduce-scatter.29.cloned.1.call-start = ((), (), s32[]{:S(2)}) async-start(), calls=%async_computation.29 | async-start | bytes 1638400 | tf_op jit(solution)/shard_map/reduce_scatter | solution.py:21
  916.5 75.5 %all-gather.37.cloned.1.call-start = ((), (), s32[]{:S(2)}) async-start(), calls=%async_computation.30 | async-start | bytes 1638400 | tf_op jit(solution)/shard_map/all_gather | solution.py:27
  960.0 68.7 %reduce-scatter.47.cloned.1.call-start = ((), (), s32[]{:S(2)}) async-start(), calls=%async_computation.39 | async-start | bytes 2621440 | tf_op jit(solution)/shard_map/reduce_scatter | solution.py:281
  965.0 102.8 %reduce-scatter.43.cloned.1.call-start = ((), (), s32[]{:S(2)}) async-start(), calls=%async_computation.37 | async-start | bytes 2621440 | tf_op jit(solution)/shard_map/reduce_scatter | solution.py:278
  970.1 125.7 %reduce-scatter.39.cloned.1.call-start = ((), (), s32[]{:S(2)}) async-start(), calls=%async_computation.35 | async-start | bytes 655360 | tf_op jit(solution)/shard_map/reduce_scatter | solution.py:275
  971.6 159.0 %reduce-scatter.35.cloned.1.call-start = ((), (), s32[]{:S(2)}) async-start(), calls=%async_computation.33 | async-start | bytes 1966080 | tf_op jit(solution)/shard_map/reduce_scatter | solution.py:272
  975.7 193.2 %reduce-scatter.45.cloned.1.call-start = ((), (), s32[]{:S(2)}) async-start(), calls=%async_computation.38 | async-start | bytes 2621440 | tf_op jit(solution)/shard_map/reduce_scatter | solution.py:281
  980.8 226.7 %reduce-scatter.41.cloned.1.call-start = ((), (), s32[]{:S(2)}) async-start(), calls=%async_computation.36 | async-start | bytes 2621440 | tf_op jit(solution)/shard_map/reduce_scatter | solution.py:278
  985.6 249.7 %reduce-scatter.37.cloned.1.call-start = ((), (), s32[]{:S(2)}) async-start(), calls=%async_computation.34 | async-start | bytes 655360 | tf_op jit(solution)/shard_map/reduce_scatter | solution.py:275
  999.4 270.0 %reduce-scatter.33.cloned.1.call-start = ((), (), s32[]{:S(2)}) async-start(), calls=%async_computation.32 | async-start | bytes 1966080 | tf_op jit(solution)/shard_map/reduce_scatter | solution.py:272
  1023.9 278.8 %reduce-scatter.31.cloned.1.call-start = ((), (), s32[]{:S(2)}) async-start(), calls=%async_computation.31 | async-start | bytes 1638400 | tf_op jit(solution)/shard_map/reduce_scatter | solution.py:21
  1026.3 276.4 %copy-start.44 = (f32[640]{0:T(1024)S(1)}, f32[640]{0:T(1024)}, u32[]{:S(2)}) copy-start(f32[640]{0:T(1024)} %copy-done.43) | copy-start | bytes 7684
  1026.3 318.6 %all-reduce.13.cloned.1.call-start = ((), (), s32[]{:S(2)}) async-start(), calls=%async_computation.46 | async-start | bytes 6291456 | tf_op jit(solution)/shard_map/psum | solution.py:286
  (96 other events, 3762.5 us)
Sparse Core Ops, SparseCore 0:
  27.2 31.6 all-gather.22
  61.3 29.4 all-gather.38
  106.1 52.0 reduce-scatter.16
  160.5 34.9 all-gather.40
  197.5 33.4 all-gather.24
  233.2 33.6 all-gather.42
  272.2 52.1 reduce-scatter.18
  326.8 33.6 all-gather.44
  362.6 32.5 all-gather.26
  421.5 50.6 reduce-scatter.20
  474.6 34.9 all-gather.46
  511.6 33.4 all-gather.28
  547.5 33.6 all-gather.48
  586.4 52.0 reduce-scatter.22
  684.6 33.3 all-gather.30
  728.0 29.7 reduce-scatter.24
  772.0 31.8 all-gather.32
  831.3 29.7 reduce-scatter.26
  874.8 31.8 all-gather.34
  916.6 29.7 reduce-scatter.28
  960.1 31.8 all-gather.36
  995.0 33.7 reduce-scatter.46
  1032.5 35.1 reduce-scatter.42
  1071.0 24.7 reduce-scatter.38
  1099.7 30.9 reduce-scatter.34
  1133.7 35.1 reduce-scatter.44
  1172.3 35.1 reduce-scatter.40
  1210.5 24.7 reduce-scatter.36
  1238.4 30.9 reduce-scatter.32
  1271.5 31.2 reduce-scatter.30
  1305.6 22.3 all-reduce.12
where the time goes:
time: 1370 us; the launch traced here: 1360 us
  waiting for transfers between devices  926 us (68%)
  blocking collectives  179 us (13%)
  matrix products  120 us (9%)
  local copies, waits for them, and re-layouts  67.1 us (5%)
  other arithmetic  45.5 us (3%)
  between operations  20.2 us (1%)
    reduce_scatter x4, waiting for transfers between devices, feature_rows(): lax.psum_scatter(partial_value, 'col', scatter_dimension=1, tiled=True)  202 us
    reduce_scatter x4, waiting for transfers between devices, gradient_rows(): lax.psum_scatter(partial_value.astype(jnp.bfloat16), 'col', scatter_dimen...  121 us
    all_gather x4, waiting for transfers between devices, norm_shares(): lax.all_gather((standard * gains + shifts).astype(jnp.bfloat16), 'col', a...  120 us
    all_gather x4, waiting for transfers between devices, gather_gradient(): return lax.all_gather(gradient, 'col', axis=1, tiled=True)  103 us
    reduce_scatter x2, waiting for transfers between devices, body(): lax.psum_scatter(up_part.astype(jnp.bfloat16), 'row', scatter_dimension=0...  77.6 us
    reduce_scatter x2, waiting for transfers between devices, body(): lax.psum_scatter(in_part.astype(jnp.bfloat16), 'row', scatter_dimension=0...  68.7 us
    reduce_scatter x2, waiting for transfers between devices, body(): lax.psum_scatter(proj_part.astype(jnp.bfloat16), 'row', scatter_dimension...  55.9 us
    all_gather x2, waiting for transfers between devices, body(): lax.all_gather(down_weight[layer_index], 'row', axis=1, tiled=True)  51.6 us
  transfers between devices with their start and end apart: 31, of which 30 were waited for; matrix products, arithmetic and copies ran while one was open for 8% of the time, Pallas kernels for 0%

commit v1 on v0

--- a/solution.py
+++ b/solution.py
@@ -180,7 +180,9 @@
     residue = current - teacher.astype(jnp.float32)
     local_squared = jnp.sum(residue * residue * row_mask)
     local_count = jnp.where(lax.axis_index("col") == 0, jnp.sum(row_mask), 0.0)
-    token_total, squared_total = lax.psum((local_count, local_squared), ("dp", "row", "col"))
+    token_total, squared_total = lax.psum(
+        lax.psum((local_count, local_squared), ("row", "col")), "dp"
+    )
     loss_value = squared_total / (token_total * model_width)
     factor = token_rows * lax.axis_size("dp") * lax.axis_size("row") / token_total
     grad_current = cotangent + 2.0 * factor * residue * row_mask

time: 1370 us -> 1370 us (level)
    psum x1 -> x2, blocking collectives: 40.1 us -> 44.2 us  [the longest x1 41.2 us: body(): lax.psum((local_count, local_squared), ('row', 'col'))]
where the time goes in v1:
time: 1370 us; the launch traced here: 1360 us
  waiting for transfers between devices  922 us (67%)
  blocking collectives  183 us (13%)
  matrix products  120 us (9%)
  local copies, waits for them, and re-layouts  67.1 us (5%)
  other arithmetic  45.5 us (3%)
  between operations  20.2 us (1%)
    reduce_scatter x4, waiting for transfers between devices, feature_rows(): lax.psum_scatter(partial_value, 'col', scatter_dimension=1, tiled=True)  202 us
    reduce_scatter x4, waiting for transfers between devices, gradient_rows(): lax.psum_scatter(partial_value.astype(jnp.bfloat16), 'col', scatter_dimen...  121 us
    all_gather x4, waiting for transfers between devices, norm_shares(): lax.all_gather((standard * gains + shifts).astype(jnp.bfloat16), 'col', a...  120 us
    all_gather x4, waiting for transfers between devices, gather_gradient(): return lax.all_gather(gradient, 'col', axis=1, tiled=True)  99.6 us
    reduce_scatter x2, waiting for transfers between devices, body(): lax.psum_scatter(up_part.astype(jnp.bfloat16), 'row', scatter_dimension=0...  77.7 us
    reduce_scatter x2, waiting for transfers between devices, body(): lax.psum_scatter(in_part.astype(jnp.bfloat16), 'row', scatter_dimension=0...  68.7 us
    reduce_scatter x2, waiting for transfers between devices, body(): lax.psum_scatter(proj_part.astype(jnp.bfloat16), 'row', scatter_dimension...  55.9 us
    all_gather x2, waiting for transfers between devices, body(): lax.all_gather(down_weight[layer_index], 'row', axis=1, tiled=True)  51.6 us
  transfers between devices with their start and end apart: 31, of which 30 were waited for; matrix products, arithmetic and copies ran while one was open for 8% of the time, Pallas kernels for 0%

profile of v1, /device:TPU:0, one launch (start us, length us, event | category | flops | bytes accessed | tf_op | source)
XLA Modules:
  0.0 1361.2 jit_solution(968919729800650335)
XLA Ops:
  11.3 13.7 %all-reduce.9 = (f32[640]{0:T(1024)S(1)}, f32[640]{0:T(1024)S(1)}) all-reduce(f32[640]{0:T(1024)S(1)} %get-tuple-element.28, f32[640]{0:T(1024)S(1)} %get-tuple-element.27), channel_id=1, replica_groups=mesh['dp'=2,'row'=4,'col'=4] {'col'}, use_global_device_ids=true, to_apply=%region_3.0 | all-reduce | flops 1280 | bytes 10240 | tf_op jit(solution)/shard_map/psum | solution.py:31
  30.8 12.9 all-gather.1
  44.3 14.6 %all-gather.23.cloned.1.call-done = bf16[640,1024]{1,0:T(8,128)(2,1)} async-done(((bf16[640,256]{1,0:T(8,128)(2,1)}), bf16[640,1024]{1,0:T(8,128)(2,1)}) %all-gather.23.cloned.1.call-update) | async-done | bytes 1310736 | tf_op jit(solution)/shard_map/all_gather | solution.py:35
  59.0 32.0 %all-gather.39.cloned.1.call-done = bf16[1,1024,3,256]{3,1,2,0:T(8,128)(2,1)} async-done(((bf16[1,256,3,256]{3,1,2,0:T(8,128)(2,1)}), bf16[1,1024,3,256]{3,1,2,0:T(8,128)(2,1)}) %all-gather.39.cloned.1.call-update) | async-done | bytes 1572880 | tf_op jit(solution)/shard_map/all_gather | solution.py:129
  107.7 50.5 %reduce-scatter.17.cloned.1.call-done = f32[640,256]{1,0:T(8,128)} async-done(((f32[640,1024]{1,0:T(8,128)}), f32[640,256]{1,0:T(8,128)}) %reduce-scatter.17.cloned.1.call-update) | async-done | bytes 655376 | tf_op jit(solution)/shard_map/reduce_scatter | solution.py:17
  174.1 21.4 %all-gather.41.cloned.1.call-done = bf16[1,1024,1024]{2,1,0:T(8,128)(2,1)} async-done(((bf16[1,256,1024]{2,1,0:T(8,128)(2,1)}), bf16[1,1024,1024]{2,1,0:T(8,128)(2,1)}) %all-gather.41.cloned.1.call-update) | async-done | bytes 2097168 | tf_op jit(solution)/shard_map/all_gather | solution.py:131
  195.6 35.5 %all-gather.25.cloned.1.call-done = bf16[640,1024]{1,0:T(8,128)(2,1)} async-done(((bf16[640,256]{1,0:T(8,128)(2,1)}), bf16[640,1024]{1,0:T(8,128)(2,1)}) %all-gather.25.cloned.1.call-update) | async-done | bytes 1310736 | tf_op jit(solution)/shard_map/all_gather | solution.py:35
  241.3 25.7 %all-gather.43.cloned.1.call-done = bf16[1,1024,1024]{2,1,0:T(8,128)(2,1)} async-done(((bf16[1,1024,256]{2,1,0:T(8,128)(2,1)}), bf16[1,1024,1024]{2,1,0:T(8,128)(2,1)}) %all-gather.43.cloned.1.call-update) | async-done | bytes 2097168 | tf_op jit(solution)/shard_map/all_gather | solution.py:132
  273.6 50.9 %reduce-scatter.19.cloned.1.call-done = f32[640,256]{1,0:T(8,128)} async-done(((f32[640,1024]{1,0:T(8,128)}), f32[640,256]{1,0:T(8,128)}) %reduce-scatter.19.cloned.1.call-update) | async-done | bytes 655376 | tf_op jit(solution)/shard_map/reduce_scatter | solution.py:17
  338.6 16.2 %all-gather.5 = bf16[1,256,1024]{2,1,0:T(8,128)(2,1)} all-gather(bf16[1,256,256]{2,1,0:T(8,128)(2,1)S(1)} %copy-done.32), channel_id=7, replica_groups=mesh['dp'=2,'row'=4,'col'=4] {'row'}, dimensions={2}, use_global_device_ids=true | all-gather | bytes 655360 | tf_op jit(solution)/shard_map/all_gather | solution.py:130
  360.5 34.7 %all-gather.27.cloned.1.call-done = bf16[640,1024]{1,0:T(8,128)(2,1)} async-done(((bf16[640,256]{1,0:T(8,128)(2,1)}), bf16[640,1024]{1,0:T(8,128)(2,1)}) %all-gather.27.cloned.1.call-update) | async-done | bytes 1310736 | tf_op jit(solution)/shard_map/all_gather | solution.py:35
  422.2 50.0 %reduce-scatter.21.cloned.1.call-done = f32[640,256]{1,0:T(8,128)} async-done(((f32[640,1024]{1,0:T(8,128)}), f32[640,256]{1,0:T(8,128)}) %reduce-scatter.21.cloned.1.call-update) | async-done | bytes 655376 | tf_op jit(solution)/shard_map/reduce_scatter | solution.py:17
  486.1 23.6 %all-gather.47.cloned.1.call-done = bf16[1,1024,1024]{2,1,0:T(8,128)(2,1)} async-done(((bf16[1,256,1024]{2,1,0:T(8,128)(2,1)}), bf16[1,1024,1024]{2,1,0:T(8,128)(2,1)}) %all-gather.47.cloned.1.call-update) | async-done | bytes 2097168 | tf_op jit(solution)/shard_map/all_gather | solution.py:131
  509.7 35.5 %all-gather.29.cloned.1.call-done = bf16[640,1024]{1,0:T(8,128)(2,1)} async-done(((bf16[640,256]{1,0:T(8,128)(2,1)}), bf16[640,1024]{1,0:T(8,128)(2,1)}) %all-gather.29.cloned.1.call-update) | async-done | bytes 1310736 | tf_op jit(solution)/shard_map/all_gather | solution.py:35
  555.4 25.9 %all-gather.49.cloned.1.call-done = bf16[1,1024,1024]{2,1,0:T(8,128)(2,1)} async-done(((bf16[1,1024,256]{2,1,0:T(8,128)(2,1)}), bf16[1,1024,1024]{2,1,0:T(8,128)(2,1)}) %all-gather.49.cloned.1.call-update) | async-done | bytes 2097168 | tf_op jit(solution)/shard_map/all_gather | solution.py:132
  588.2 50.3 %reduce-scatter.23.cloned.1.call-done = f32[640,256]{1,0:T(8,128)} async-done(((f32[640,1024]{1,0:T(8,128)}), f32[640,256]{1,0:T(8,128)}) %reduce-scatter.23.cloned.1.call-update) | async-done | bytes 655376 | tf_op jit(solution)/shard_map/reduce_scatter | solution.py:17
  641.4 41.2 %all-reduce = (f32[]{:T(128)}, f32[]{:T(128)}) all-reduce(f32[]{:T(128)} %get-tuple-element.92, f32[]{:T(128)S(6)} %select_n.15), channel_id=1, replica_groups=mesh['dp'=2,'row'=4,'col'=4] {'row','col'}, use_global_device_ids=true, to_apply=%region_25.26 | all-reduce | flops 2 | bytes 16 | tf_op jit(solution)/shard_map/psum | solution.py:184
  688.7 29.8 %all-gather.31.cloned.1.call-done = bf16[640,1024]{1,0:T(8,128)(2,1)} async-done(((bf16[640,256]{1,0:T(8,128)(2,1)}), bf16[640,1024]{1,0:T(8,128)(2,1)}) %all-gather.31.cloned.1.call-update) | async-done | bytes 1310736 | tf_op jit(solution)/shard_map/all_gather | solution.py:27
  728.4 29.8 %reduce-scatter.25.cloned.1.call-done = bf16[640,256]{1,0:T(8,128)(2,1)} async-done(((bf16[640,1024]{1,0:T(8,128)(2,1)}), bf16[640,256]{1,0:T(8,128)(2,1)}) %reduce-scatter.25.cloned.1.call-update) | async-done | bytes 327696 | tf_op jit(solution)/shard_map/reduce_scatter | solution.py:21
  772.6 31.7 %all-gather.33.cloned.1.call-done = bf16[640,1024]{1,0:T(8,128)(2,1)} async-done(((bf16[640,256]{1,0:T(8,128)(2,1)}), bf16[640,1024]{1,0:T(8,128)(2,1)}) %all-gather.33.cloned.1.call-update) | async-done | bytes 1310736 | tf_op jit(solution)/shard_map/all_gather | solution.py:27
  831.7 29.8 %reduce-scatter.27.cloned.1.call-done = bf16[640,256]{1,0:T(8,128)(2,1)} async-done(((bf16[640,1024]{1,0:T(8,128)(2,1)}), bf16[640,256]{1,0:T(8,128)(2,1)}) %reduce-scatter.27.cloned.1.call-update) | async-done | bytes 327696 | tf_op jit(solution)/shard_map/reduce_scatter | solution.py:21
  875.5 31.7 %all-gather.35.cloned.1.call-done = bf16[640,1024]{1,0:T(8,128)(2,1)} async-done(((bf16[640,256]{1,0:T(8,128)(2,1)}), bf16[640,1024]{1,0:T(8,128)(2,1)}) %all-gather.35.cloned.1.call-update) | async-done | bytes 1310736 | tf_op jit(solution)/shard_map/all_gather | solution.py:27
  917.1 29.9 %reduce-scatter.29.cloned.1.call-done = bf16[640,256]{1,0:T(8,128)(2,1)} async-done(((bf16[640,1024]{1,0:T(8,128)(2,1)}), bf16[640,256]{1,0:T(8,128)(2,1)}) %reduce-scatter.29.cloned.1.call-update) | async-done | bytes 327696 | tf_op jit(solution)/shard_map/reduce_scatter | solution.py:21
  1029.2 39.1 %reduce-scatter.43.cloned.1.call-done = bf16[256,1024]{1,0:T(8,128)(2,1)} async-done(((bf16[1024,1024]{1,0:T(8,128)(2,1)}), bf16[256,1024]{1,0:T(8,128)(2,1)}) %reduce-scatter.43.cloned.1.call-update) | async-done | bytes 524304 | tf_op jit(solution)/shard_map/reduce_scatter | solution.py:280
  1068.3 28.1 %reduce-scatter.39.cloned.1.call-done = bf16[256,256]{1,0:T(8,128)(2,1)} async-done(((bf16[256,1024]{1,0:T(8,128)(2,1)}), bf16[256,256]{1,0:T(8,128)(2,1)}) %reduce-scatter.39.cloned.1.call-update) | async-done | bytes 131088 | tf_op jit(solution)/shard_map/reduce_scatter | solution.py:277
  1096.3 34.8 %reduce-scatter.35.cloned.1.call-done = bf16[256,3,256]{2,0,1:T(8,128)(2,1)} async-done(((bf16[1024,3,256]{2,0,1:T(8,128)(2,1)}), bf16[256,3,256]{2,0,1:T(8,128)(2,1)}) %reduce-scatter.35.cloned.1.call-update) | async-done | bytes 393232 | tf_op jit(solution)/shard_map/reduce_scatter | solution.py:274
  1131.1 38.3 %reduce-scatter.45.cloned.1.call-done = bf16[1024,256]{1,0:T(8,128)(2,1)} async-done(((bf16[1024,1024]{1,0:T(8,128)(2,1)}), bf16[1024,256]{1,0:T(8,128)(2,1)}) %reduce-scatter.45.cloned.1.call-update) | async-done | bytes 524304 | tf_op jit(solution)/shard_map/reduce_scatter | solution.py:283
  1169.4 38.6 %reduce-scatter.41.cloned.1.call-done = bf16[256,1024]{1,0:T(8,128)(2,1)} async-done(((bf16[1024,1024]{1,0:T(8,128)(2,1)}), bf16[256,1024]{1,0:T(8,128)(2,1)}) %reduce-scatter.41.cloned.1.call-update) | async-done | bytes 524304 | tf_op jit(solution)/shard_map/reduce_scatter | solution.py:280
  1208.0 27.9 %reduce-scatter.37.cloned.1.call-done = bf16[256,256]{1,0:T(8,128)(2,1)} async-done(((bf16[256,1024]{1,0:T(8,128)(2,1)}), bf16[256,256]{1,0:T(8,128)(2,1)}) %reduce-scatter.37.cloned.1.call-update) | async-done | bytes 131088 | tf_op jit(solution)/shard_map/reduce_scatter | solution.py:277
  1235.9 33.9 %reduce-scatter.33.cloned.1.call-done = bf16[256,3,256]{2,0,1:T(8,128)(2,1)} async-done(((bf16[1024,3,256]{2,0,1:T(8,128)(2,1)}), bf16[256,3,256]{2,0,1:T(8,128)(2,1)}) %reduce-scatter.33.cloned.1.call-update) | async-done | bytes 393232 | tf_op jit(solution)/shard_map/reduce_scatter | solution.py:274
  1271.8 31.4 %reduce-scatter.31.cloned.1.call-done = bf16[640,256]{1,0:T(8,128)(2,1)} async-done(((bf16[640,1024]{1,0:T(8,128)(2,1)}), bf16[640,256]{1,0:T(8,128)(2,1)}) %reduce-scatter.31.cloned.1.call-update) | async-done | bytes 327696 | tf_op jit(solution)/shard_map/reduce_scatter | solution.py:21
  1304.7 26.5 %all-reduce.1 = (f32[1,2,256]{2,1,0:T(2,128)S(1)}, f32[1,2,256]{2,1,0:T(2,128)S(1)}, f32[1,2,256]{2,1,0:T(2,128)S(1)}, f32[1,2,256]{2,1,0:T(2,128)S(1)}, f32[1,2...) all-reduce(f32[1,2,256]{2,1,0:T(2,128)S(1)} %maximum_bitcast_fusion, ...), channel_id=1, replica_groups=mesh['dp'=2,'row'=4,'col'=4] {'dp','row'}, use_global_device_ids=true, to_apply=%region_57.58 | all-reduce | flops 6144 | bytes 49152 | tf_op jit(solution)/shard_map/psum | solution.py:293
  (411 shorter events, 325.2 us)
Async XLA Ops:
  7.2 51.7 %all-gather.23.cloned.1.call-start = ((), (), s32[]{:S(2)}) async-start(), calls=%async_computation.16 | async-start | bytes 1638400 | tf_op jit(solution)/shard_map/all_gather | solution.py:35
  27.1 63.8 %all-gather.39.cloned.1.call-start = ((), (), s32[]{:S(2)}) async-start(), calls=%async_computation.40 | async-start | bytes 1966080 | tf_op jit(solution)/shard_map/all_gather | solution.py:129
  29.3 129.0 %reduce-scatter.17.cloned.1.call-start = ((), (), s32[]{:S(2)}) async-start(), calls=%async_computation.17 | async-start | bytes 3276800 | tf_op jit(solution)/shard_map/reduce_scatter | solution.py:17
  106.0 89.5 %all-gather.41.cloned.1.call-start = ((), (), s32[]{:S(2)}) async-start(), calls=%async_computation.41 | async-start | bytes 2621440 | tf_op jit(solution)/shard_map/all_gather | solution.py:131
  107.2 123.9 %all-gather.25.cloned.1.call-start = ((), (), s32[]{:S(2)}) async-start(), calls=%async_computation.18 | async-start | bytes 1638400 | tf_op jit(solution)/shard_map/all_gather | solution.py:35
  170.9 96.1 %all-gather.43.cloned.1.call-start = ((), (), s32[]{:S(2)}) async-start(), calls=%async_computation.42 | async-start | bytes 2621440 | tf_op jit(solution)/shard_map/all_gather | solution.py:132
  173.2 151.2 %reduce-scatter.19.cloned.1.call-start = ((), (), s32[]{:S(2)}) async-start(), calls=%async_computation.19 | async-start | bytes 3276800 | tf_op jit(solution)/shard_map/reduce_scatter | solution.py:17
  272.1 88.4 %all-gather.45.cloned.1.call-start = ((), (), s32[]{:S(2)}) async-start(), calls=%async_computation.43 | async-start | bytes 1966080 | tf_op jit(solution)/shard_map/all_gather | solution.py:129
  272.9 122.4 %all-gather.27.cloned.1.call-start = ((), (), s32[]{:S(2)}) async-start(), calls=%async_computation.20 | async-start | bytes 1638400 | tf_op jit(solution)/shard_map/all_gather | solution.py:35
  337.2 135.0 %reduce-scatter.21.cloned.1.call-start = ((), (), s32[]{:S(2)}) async-start(), calls=%async_computation.21 | async-start | bytes 3276800 | tf_op jit(solution)/shard_map/reduce_scatter | solution.py:17
  421.4 88.2 %all-gather.47.cloned.1.call-start = ((), (), s32[]{:S(2)}) async-start(), calls=%async_computation.44 | async-start | bytes 2621440 | tf_op jit(solution)/shard_map/all_gather | solution.py:131
  422.2 123.0 %all-gather.29.cloned.1.call-start = ((), (), s32[]{:S(2)}) async-start(), calls=%async_computation.22 | async-start | bytes 1638400 | tf_op jit(solution)/shard_map/all_gather | solution.py:35
  484.8 96.4 %all-gather.49.cloned.1.call-start = ((), (), s32[]{:S(2)}) async-start(), calls=%async_computation.45 | async-start | bytes 2621440 | tf_op jit(solution)/shard_map/all_gather | solution.py:132
  485.6 152.9 %reduce-scatter.23.cloned.1.call-start = ((), (), s32[]{:S(2)}) async-start(), calls=%async_computation.23 | async-start | bytes 3276800 | tf_op jit(solution)/shard_map/reduce_scatter | solution.py:17
  586.3 132.3 %all-gather.31.cloned.1.call-start = ((), (), s32[]{:S(2)}) async-start(), calls=%async_computation.24 | async-start | bytes 1638400 | tf_op jit(solution)/shard_map/all_gather | solution.py:27
  688.6 69.6 %reduce-scatter.25.cloned.1.call-start = ((), (), s32[]{:S(2)}) async-start(), calls=%async_computation.25 | async-start | bytes 1638400 | tf_op jit(solution)/shard_map/reduce_scatter | solution.py:21
  728.3 76.0 %all-gather.33.cloned.1.call-start = ((), (), s32[]{:S(2)}) async-start(), calls=%async_computation.26 | async-start | bytes 1638400 | tf_op jit(solution)/shard_map/all_gather | solution.py:27
  772.3 89.3 %reduce-scatter.27.cloned.1.call-start = ((), (), s32[]{:S(2)}) async-start(), calls=%async_computation.27 | async-start | bytes 1638400 | tf_op jit(solution)/shard_map/reduce_scatter | solution.py:21
  831.7 75.5 %all-gather.35.cloned.1.call-start = ((), (), s32[]{:S(2)}) async-start(), calls=%async_computation.28 | async-start | bytes 1638400 | tf_op jit(solution)/shard_map/all_gather | solution.py:27
  875.2 71.7 %reduce-scatter.29.cloned.1.call-start = ((), (), s32[]{:S(2)}) async-start(), calls=%async_computation.29 | async-start | bytes 1638400 | tf_op jit(solution)/shard_map/reduce_scatter | solution.py:21
  917.0 75.5 %all-gather.37.cloned.1.call-start = ((), (), s32[]{:S(2)}) async-start(), calls=%async_computation.30 | async-start | bytes 1638400 | tf_op jit(solution)/shard_map/all_gather | solution.py:27
  960.5 68.7 %reduce-scatter.47.cloned.1.call-start = ((), (), s32[]{:S(2)}) async-start(), calls=%async_computation.39 | async-start | bytes 2621440 | tf_op jit(solution)/shard_map/reduce_scatter | solution.py:283
  965.5 102.8 %reduce-scatter.43.cloned.1.call-start = ((), (), s32[]{:S(2)}) async-start(), calls=%async_computation.37 | async-start | bytes 2621440 | tf_op jit(solution)/shard_map/reduce_scatter | solution.py:280
  970.6 125.7 %reduce-scatter.39.cloned.1.call-start = ((), (), s32[]{:S(2)}) async-start(), calls=%async_computation.35 | async-start | bytes 655360 | tf_op jit(solution)/shard_map/reduce_scatter | solution.py:277
  972.1 159.0 %reduce-scatter.35.cloned.1.call-start = ((), (), s32[]{:S(2)}) async-start(), calls=%async_computation.33 | async-start | bytes 1966080 | tf_op jit(solution)/shard_map/reduce_scatter | solution.py:274
  976.2 193.2 %reduce-scatter.45.cloned.1.call-start = ((), (), s32[]{:S(2)}) async-start(), calls=%async_computation.38 | async-start | bytes 2621440 | tf_op jit(solution)/shard_map/reduce_scatter | solution.py:283
  981.3 226.7 %reduce-scatter.41.cloned.1.call-start = ((), (), s32[]{:S(2)}) async-start(), calls=%async_computation.36 | async-start | bytes 2621440 | tf_op jit(solution)/shard_map/reduce_scatter | solution.py:280
  986.1 249.8 %reduce-scatter.37.cloned.1.call-start = ((), (), s32[]{:S(2)}) async-start(), calls=%async_computation.34 | async-start | bytes 655360 | tf_op jit(solution)/shard_map/reduce_scatter | solution.py:277
  999.9 269.9 %reduce-scatter.33.cloned.1.call-start = ((), (), s32[]{:S(2)}) async-start(), calls=%async_computation.32 | async-start | bytes 1966080 | tf_op jit(solution)/shard_map/reduce_scatter | solution.py:274
  1024.4 278.8 %reduce-scatter.31.cloned.1.call-start = ((), (), s32[]{:S(2)}) async-start(), calls=%async_computation.31 | async-start | bytes 1638400 | tf_op jit(solution)/shard_map/reduce_scatter | solution.py:21
  1026.8 276.4 %copy-start.44 = (f32[640]{0:T(1024)S(1)}, f32[640]{0:T(1024)}, u32[]{:S(2)}) copy-start(f32[640]{0:T(1024)} %copy-done.43) | copy-start | bytes 7684
  1026.9 318.6 %all-reduce.14.cloned.1.call-start = ((), (), s32[]{:S(2)}) async-start(), calls=%async_computation.46 | async-start | bytes 6291456 | tf_op jit(solution)/shard_map/psum | solution.py:288
  (96 other events, 3762.3 us)
Sparse Core Ops, SparseCore 0:
  27.3 31.6 all-gather.22
  61.4 29.4 all-gather.38
  106.1 52.0 reduce-scatter.16
  160.6 34.9 all-gather.40
  197.5 33.4 all-gather.24
  233.3 33.6 all-gather.42
  272.2 52.1 reduce-scatter.18
  326.9 33.6 all-gather.44
  362.7 32.5 all-gather.26
  421.5 50.6 reduce-scatter.20
  474.6 34.9 all-gather.46
  511.6 33.4 all-gather.28
  547.5 33.6 all-gather.48
  586.4 52.0 reduce-scatter.22
  688.7 29.7 all-gather.30
  728.4 29.7 reduce-scatter.24
  772.4 31.8 all-gather.32
  831.8 29.7 reduce-scatter.26
  875.3 31.8 all-gather.34
  917.2 29.7 reduce-scatter.28
  960.6 31.8 all-gather.36
  995.5 33.7 reduce-scatter.46
  1033.0 35.2 reduce-scatter.42
  1071.5 24.7 reduce-scatter.38
  1100.2 30.9 reduce-scatter.34
  1134.2 35.1 reduce-scatter.44
  1172.8 35.1 reduce-scatter.40
  1211.1 24.7 reduce-scatter.36
  1238.9 30.8 reduce-scatter.32
  1271.9 31.2 reduce-scatter.30
  1306.1 22.3 all-reduce.13
